TPU v7x, 128 devices: a whole 4x4x4 slice. The times are simulated.
128 devices in a mesh: dp: 2 (over y_hi), fsdp: 64 (over y_lo, z, x, core).
Axes of the slice: x: 4, y: 4 (y_hi: 2, y_lo: 2; y = y_hi * 2 + y_lo), z: 4, core: 2. Of those that a mesh axis runs over, the one named last changes fastest.
Arguments:
- tokens: bfloat16 [65536, 768], P(('dp', 'fsdp')), may hold values from -6 to 6
- lengths: int32 [128, 16], replicated, may hold values from 1 to 64, as said below
- ln1_gain: bfloat16 [768], P('fsdp'), may hold values from 0.5 to 1.5
- ln1_bias: bfloat16 [768], P('fsdp'), may hold values from -3 to 3
- w_qkv: bfloat16 [768, 2304], P('fsdp'), may hold values from -0.21875 to 0.21875
- q_bias: bfloat16 [768], P('fsdp'), may hold values from -3 to 3
- v_bias: bfloat16 [768], P('fsdp'), may hold values from -3 to 3
- w_out: bfloat16 [768, 768], P('fsdp'), may hold values from -1.25 to 1.25
- out_bias: bfloat16 [768], P('fsdp'), may hold values from -3 to 3
- ln2_gain: bfloat16 [768], P('fsdp'), may hold values from 0.5 to 1.5
- ln2_bias: bfloat16 [768], P('fsdp'), may hold values from -3 to 3
- w_in: bfloat16 [768, 3072], P('fsdp'), may hold values from -0.21875 to 0.21875
- in_bias: bfloat16 [3072], P('fsdp'), may hold values from -3 to 3
- w_back: bfloat16 [3072, 768], P('fsdp'), may hold values from -0.15625 to 0.15625
- back_bias: bfloat16 [768], P('fsdp'), may hold values from -3 to 3
- cotangent: bfloat16 [65536, 768], P(('dp', 'fsdp')), may hold values from -6 to 6
Outputs:
- hidden: bfloat16 [65536, 768], P(('dp', 'fsdp'))
- input_grad: float32 [65536, 768], P(('dp', 'fsdp'))
- ln1_gain_grad: float32 [768], P('fsdp')
- ln1_bias_grad: float32 [768], P('fsdp')
- w_qkv_grad: float32 [768, 2304], P('fsdp')
- q_bias_grad: float32 [768], P('fsdp')
- v_bias_grad: float32 [768], P('fsdp')
- w_out_grad: float32 [768, 768], P('fsdp')
- out_bias_grad: float32 [768], P('fsdp')
- ln2_gain_grad: float32 [768], P('fsdp')
- ln2_bias_grad: float32 [768], P('fsdp')
- w_in_grad: float32 [768, 3072], P('fsdp')
- in_bias_grad: float32 [3072], P('fsdp')
- w_back_grad: float32 [3072, 768], P('fsdp')
- back_bias_grad: float32 [768], P('fsdp')
Inputs may be any that keep to these rules, and one draw needn't show every extreme that they name: Each row holds the 16 caption lengths of one packed sequence, adding up to 512; every row's longest caption is exactly 64.
All inputs are finite; a program needn't handle non-finite values.
Results may differ from a plain program's by a relative error of at most 0.012.
Values may be sent and summed in bfloat16 or wider, within the bound.
No kernel may reach another device: no remote copies, remote signals or barrier semaphores. Data moves between devices by JAX's collectives and lax.ppermute only.
A program may use at most 192 MiB of HBM per device.

v0:
```python
import jax
import jax.numpy as jnp
from jax import lax
from jax.sharding import PartitionSpec as P

HEADS = 12
HEAD_DIM = 64
LEN = 512
SEQS = 1


def for_sending(array):
    return jax.tree.map(lambda a: a.astype(jnp.bfloat16) if a.dtype == jnp.float32 else a, array)


def in_blocks(array, dim, devices):
    lengths = array.shape
    pieces = array.reshape(*lengths[:dim], devices, lengths[dim] // devices, *lengths[dim + 1 :])
    return jnp.moveaxis(pieces, dim, 0)


def sum_packed(arrays, axis, dims):
    devices = lax.axis_size(axis)
    pieces = [in_blocks(a, dim, devices) for a, dim in zip(arrays, dims)]
    lines = jnp.concatenate([b.reshape(devices, -1) for b in pieces], axis=1)
    extent = max(16, -(-lines.shape[1] // 1024) * 8)
    lines = jnp.pad(lines, ((0, 0), (0, extent * 128 - lines.shape[1]))).reshape(-1, 128)
    line, at, done = (lax.psum_scatter(lines, axis, tiled=True).reshape(-1), 0, [])
    for b in pieces:
        part = b[0]
        done.append(line[at : at + part.size].reshape(part.shape))
        at += part.size
    return tuple(done)


def from_everyone(array, axis):
    copies = jnp.broadcast_to(array, (lax.axis_size(axis), *array.shape))
    return lax.all_to_all(copies, axis, split_axis=0, concat_axis=0, tiled=True)


def of_everyone(array, axis):
    return from_everyone(array, axis).sum(axis=0)


def in_one(arrays, axis):
    ends = [0]
    for a in arrays:
        ends.append(ends[-1] + a.size)
    total = of_everyone(jnp.concatenate([a.ravel() for a in arrays]), axis)
    return tuple((total[b:e].reshape(a.shape) for a, b, e in zip(arrays, ends, ends[1:])))


def layer_norm(values, gain, shift):
    centre = values - jnp.mean(values, axis=-1, keepdims=True)
    scale = lax.rsqrt(jnp.mean(centre * centre, axis=-1, keepdims=True) + 1e-05)
    normed = centre * scale
    return (normed * gain + shift, normed, scale)


def norm_back(d_out, normed, scale, gain):
    gain_grad = jnp.sum(d_out * normed, axis=0)
    shift_grad = jnp.sum(d_out, axis=0)
    expand = d_out * gain
    d_in = scale * (
        expand
        - jnp.mean(expand, axis=-1, keepdims=True)
        - normed * jnp.mean(expand * normed, axis=-1, keepdims=True)
    )
    return (d_in, gain_grad, shift_grad)


def caption_ids(lengths, device):
    lens = lax.dynamic_slice_in_dim(lengths, device * SEQS, SEQS, 0)
    ends = jnp.cumsum(lens, axis=1)
    place = jnp.arange(LEN, dtype=jnp.int32)
    return jnp.sum((ends[:, None, :] <= place[None, :, None]).astype(jnp.int32), axis=-1)


def fetch(params):
    return jax.tree.map(
        lambda part, own: part.astype(own.dtype),
        lax.all_gather(for_sending(params), "fsdp", axis=0, tiled=True),
        params,
    )


def attention_probs(query, keys, allowed, logsum):
    scores = jnp.einsum(
        "qhd,khd->hqk", query, keys, preferred_element_type=jnp.float32
    ) * HEAD_DIM ** (-0.5)
    scores = jnp.where(allowed[None], scores, -1e30)
    if logsum is None:
        top = jnp.max(scores, axis=-1, keepdims=True)
        logsum = top + jnp.log(jnp.sum(jnp.exp(scores - top), axis=-1, keepdims=True))
    return (jnp.exp(scores - logsum), logsum)


def attend(item):
    query, keys, vals, ids = item
    allowed = ids[:, None] == ids[None, :]
    probs, logsum = attention_probs(query, keys, allowed, None)
    mixed = jnp.einsum(
        "hqk,khd->qhd", probs.astype(jnp.bfloat16), vals, preferred_element_type=jnp.float32
    ).astype(jnp.bfloat16)
    return (mixed, logsum)


def attend_back(item):
    query, keys, vals, ids, logsum, d_mixed = item
    allowed = ids[:, None] == ids[None, :]
    probs, unused = attention_probs(query, keys, allowed, logsum)
    d_probs = jnp.einsum("qhd,khd->hqk", d_mixed, vals, preferred_element_type=jnp.float32)
    d_scores = (probs * (d_probs - jnp.sum(probs * d_probs, axis=-1, keepdims=True))).astype(
        jnp.bfloat16
    )
    d_query = jnp.einsum(
        "hqk,khd->qhd", d_scores, keys, preferred_element_type=jnp.float32
    ) * HEAD_DIM ** (-0.5)
    d_keys = jnp.einsum(
        "hqk,qhd->khd", d_scores, query, preferred_element_type=jnp.float32
    ) * HEAD_DIM ** (-0.5)
    d_vals = jnp.einsum(
        "hqk,qhd->khd", probs.astype(jnp.bfloat16), d_mixed, preferred_element_type=jnp.float32
    )
    return (d_query, d_keys, d_vals)


def forward(values, full, ids):
    g1, s1, wqkv, qb, vb, wo, ob, g2, s2, w1, bi1, w2, b2 = full
    rows, width = values.shape
    seqs = rows // LEN
    normed_out, normed1, scale1 = layer_norm(values, g1.astype(jnp.float32), s1.astype(jnp.float32))
    act1 = normed_out.astype(jnp.bfloat16)
    bias_all = jnp.concatenate(
        [qb.astype(jnp.float32), jnp.zeros((width,), jnp.float32), vb.astype(jnp.float32)]
    )
    proj = (jnp.dot(act1, wqkv, preferred_element_type=jnp.float32) + bias_all).astype(jnp.bfloat16)
    query = proj[:, :width].reshape(seqs, LEN, HEADS, HEAD_DIM)
    keys = proj[:, width : 2 * width].reshape(seqs, LEN, HEADS, HEAD_DIM)
    vals = proj[:, 2 * width :].reshape(seqs, LEN, HEADS, HEAD_DIM)
    mixed, logsum = lax.map(attend, (query, keys, vals, ids))
    mixed = mixed.reshape(rows, width)
    middle = (
        values + jnp.dot(mixed, wo, preferred_element_type=jnp.float32) + ob.astype(jnp.float32)
    )
    normed_out2, normed2, scale2 = layer_norm(
        middle, g2.astype(jnp.float32), s2.astype(jnp.float32)
    )
    act2 = normed_out2.astype(jnp.bfloat16)
    pre = jnp.dot(act2, w1, preferred_element_type=jnp.float32) + bi1.astype(jnp.float32)
    gact = jax.nn.gelu(pre, approximate=False).astype(jnp.bfloat16)
    result = middle + jnp.dot(gact, w2, preferred_element_type=jnp.float32) + b2.astype(jnp.float32)
    kept = (
        normed1,
        scale1,
        act1,
        query,
        keys,
        vals,
        logsum,
        mixed,
        normed2,
        scale2,
        act2,
        pre,
        gact,
    )
    return (result, kept)


def backward(d_result, full, ids, kept):
    g1, s1, wqkv, qb, vb, wo, ob, g2, s2, w1, bi1, w2, b2 = full
    normed1, scale1, act1, query, keys, vals, logsum, mixed, normed2, scale2, act2, pre, gact = kept
    rows, width = d_result.shape
    seqs = rows // LEN
    d_up = d_result.astype(jnp.bfloat16)
    grad_w2 = jnp.einsum("ti,tj->ij", gact, d_up, preferred_element_type=jnp.float32)
    grad_b2 = jnp.sum(d_up.astype(jnp.float32), axis=0)
    d_gact = jnp.einsum("tj,ij->ti", d_up, w2, preferred_element_type=jnp.float32)
    d_pre = jax.vjp(lambda arg: jax.nn.gelu(arg, approximate=False), pre)[1](d_gact)[0].astype(
        jnp.bfloat16
    )
    grad_bi1 = jnp.sum(d_pre.astype(jnp.float32), axis=0)
    grad_w1 = jnp.einsum("ti,tj->ij", act2, d_pre, preferred_element_type=jnp.float32)
    d_act2 = jnp.einsum("tj,ij->ti", d_pre, w1, preferred_element_type=jnp.float32)
    d_mid_ln, grad_g2, grad_s2 = norm_back(d_act2, normed2, scale2, g2.astype(jnp.float32))
    d_middle = d_result + d_mid_ln
    d_branch = d_middle.astype(jnp.bfloat16)
    grad_wo = jnp.einsum("ti,tj->ij", mixed, d_branch, preferred_element_type=jnp.float32)
    grad_ob = jnp.sum(d_branch.astype(jnp.float32), axis=0)
    d_mixed = (
        jnp.einsum("tj,ij->ti", d_branch, wo, preferred_element_type=jnp.float32)
        .astype(jnp.bfloat16)
        .reshape(seqs, LEN, HEADS, HEAD_DIM)
    )
    d_query, d_keys, d_vals = lax.map(attend_back, (query, keys, vals, ids, logsum, d_mixed))
    d_proj = jnp.concatenate(
        [d_query.reshape(rows, width), d_keys.reshape(rows, width), d_vals.reshape(rows, width)],
        axis=1,
    ).astype(jnp.bfloat16)
    d_proj_wide = d_proj.astype(jnp.float32)
    grad_qb = jnp.sum(d_proj_wide[:, :width], axis=0)
    grad_vb = jnp.sum(d_proj_wide[:, 2 * width :], axis=0)
    grad_wqkv = jnp.einsum("ti,tj->ij", act1, d_proj, preferred_element_type=jnp.float32)
    d_act1 = jnp.einsum("tj,ij->ti", d_proj, wqkv, preferred_element_type=jnp.float32)
    d_in_ln, grad_g1, grad_s1 = norm_back(d_act1, normed1, scale1, g1.astype(jnp.float32))
    d_input = d_middle + d_in_ln
    grads = (
        grad_g1,
        grad_s1,
        grad_wqkv,
        grad_qb,
        grad_vb,
        grad_wo,
        grad_ob,
        grad_g2,
        grad_s2,
        grad_w1,
        grad_bi1,
        grad_w2,
        grad_b2,
    )
    return (d_input, grads)


def shards(
    tokens,
    lengths,
    ln1_gain,
    ln1_bias,
    w_qkv,
    q_bias,
    v_bias,
    w_out,
    out_bias,
    ln2_gain,
    ln2_bias,
    w_in,
    in_bias,
    w_back,
    back_bias,
    cotangent,
):
    params = (
        ln1_gain,
        ln1_bias,
        w_qkv,
        q_bias,
        v_bias,
        w_out,
        out_bias,
        ln2_gain,
        ln2_bias,
        w_in,
        in_bias,
        w_back,
        back_bias,
    )
    device = lax.axis_index("dp") * lax.axis_size("fsdp") + lax.axis_index("fsdp")
    ids = caption_ids(lengths, device)
    values = tokens.astype(jnp.float32)
    full = fetch(params)
    result, unused = forward(values, full, ids)
    again = fetch(params)
    redone, kept = forward(values, again, ids)
    d_input, grads = backward(cotangent.astype(jnp.float32), again, ids, kept)
    shares = sum_packed(
        (
            grads[0],
            grads[1],
            grads[2],
            grads[3],
            grads[4],
            grads[5],
            grads[6],
            grads[7],
            grads[8],
            grads[9],
            grads[10],
            grads[11],
            grads[12],
        ),
        "fsdp",
        (0, 0, 0, 0, 0, 0, 0, 0, 0, 0, 0, 0, 0),
    )
    summed = in_one(
        (
            shares[0],
            shares[1],
            shares[2],
            shares[3],
            shares[4],
            shares[5],
            shares[6],
            shares[7],
            shares[8],
            shares[9],
            shares[10],
            shares[11],
            shares[12],
        ),
        "dp",
    )
    return (
        result.astype(jnp.bfloat16),
        d_input,
        summed[0],
        summed[1],
        summed[2],
        summed[3],
        summed[4],
        summed[5],
        summed[6],
        summed[7],
        summed[8],
        summed[9],
        summed[10],
        summed[11],
        summed[12],
    )


def solution(mesh):
    placed = (
        P(("dp", "fsdp"), None),
        P(),
        P("fsdp"),
        P("fsdp"),
        P("fsdp", None),
        P("fsdp"),
        P("fsdp"),
        P("fsdp", None),
        P("fsdp"),
        P("fsdp"),
        P("fsdp"),
        P("fsdp", None),
        P("fsdp"),
        P("fsdp", None),
        P("fsdp"),
        P(("dp", "fsdp"), None),
    )
    return jax.shard_map(
        shards,
        mesh=mesh,
        in_specs=placed,
        out_specs=(
            P(("dp", "fsdp"), None),
            P(("dp", "fsdp"), None),
            P("fsdp"),
            P("fsdp"),
            P("fsdp", None),
            P("fsdp"),
            P("fsdp"),
            P("fsdp", None),
            P("fsdp"),
            P("fsdp"),
            P("fsdp"),
            P("fsdp", None),
            P("fsdp"),
            P("fsdp", None),
            P("fsdp"),
        ),
        check_vma=False,
    )
```

profile of v0, /device:TPU:0, one launch (start us, length us, event | category | flops | bytes accessed | tf_op | source)
XLA Modules:
  0.0 1075.4 jit_solution(6866785027595328660)
XLA Ops:
  20.2 282.3 %all-reduce.11 = (bf16[768]{0:T(1024)(128)(2,1)S(1)}, bf16[768]{0:T(1024)(128)(2,1)S(1)}, bf16[768]{0:T(1024)(128)(2,1)S(1)}, bf16[768]{0:T(1024)(128)(2,1)S(1)}...) all-reduce(bf16[768]{0:T(1024)(128)(2,1)S(1)} %dynamic-update-slice, ...), channel_id=1, replica_groups=mesh['dp'=2,'fsdp'=64] {'fsdp'}, use_global_device_ids=true, to_apply=%add.4 | all-reduce | flops 9216 | bytes 36864
  306.1 3.2 reshape.295
  309.3 6.5 reshape.293
  315.8 4.2 fusion.8
  329.6 3.2 convolution_convert_fusion.2
  335.3 19.8 %reshape.297 = bf16[768,3072]{1,0:T(8,128)(2,1)} reshape(bf16[64,12,3072]{2,1,0:T(8,128)(2,1)} %all-gather.14.cloned.1.call-done) | data formatting | bytes 9437184
  355.1 7.1 fusion.39
  362.2 77.9 %all-gather.8.cloned.1.call-done = bf16[3072,768]{1,0:T(8,128)(2,1)} async-done(((bf16[48,768]{1,0:T(8,128)(2,1)}), bf16[3072,768]{1,0:T(8,128)(2,1)}) %all-gather.8.cloned.1.call-update) | async-done | bytes 4718608 | tf_op jit(solution)/shard_map/all_gather | solution.py:82
  440.1 20.1 %convert_reduce_fusion = (f32[3072]{0:T(1024)S(1)}, bf16[512,3072]{1,0:T(8,128)(2,1)S(1)}, f32[512,3072]{1,0:T(8,128)}) fusion(f32[512,3072]{1,0:T(8,128)} %fusion.39, f32[3072]{0:T(1024)S(1)} %convert_element_type.132, bf16[512,768]{1,0:T(8,128)(2,1)} %param.31, bf16[3072,768]{1,0:T(8,128)(2,1)} %all-gather.8.cloned.1.call-done), kind=kOutput, calls=%fused_computation.9 | convolution fusion | flops 2533880832 | bytes 21258240 | tf_op jit(solution)/shard_map/tj,ij->ti/dot_general | solution.py:179
  468.6 9.0 convolution_convert_fusion.1
  477.6 9.5 multiply_reduce_fusion
  487.1 6.8 multiply_convert_fusion
  498.3 4.0 fusion.21
  502.3 5.2 fusion.33
  512.8 5.7 fusion.38
  518.6 3.2 multiply_convert_fusion.1
  522.0 7.2 reshape_reshape.12
  531.5 3.1 reshape_reshape.13
  534.9 11.8 %reshape_reshape.14 = f32[64,36864]{1,0:T(8,128)} reshape(f32[768,3072]{1,0:T(8,128)} %fusion.38) | data formatting | bytes 18874368 | tf_op jit(solution)/shard_map/reshape;reshape | solution.py:25
  546.8 8.1 fusion.45
  554.9 10.0 reshape_reshape.15
  568.1 23.2 %dynamic-update-slice.11 = f32[64,110736]{1,0:T(8,128)} dynamic-update-slice(f32[64,110736]{1,0:T(8,128)} %dynamic-update-slice.10, f32[64,27648]{1,0:T(8,128)} %reshape_reshape.12, s32[]{} %constant.235, s32[]{} %constant.237) | dynamic-update-slice | bytes 14155780
  594.5 12.1 %dynamic-update-slice.14 = f32[64,110736]{1,0:T(8,128)} dynamic-update-slice(f32[64,110736]{1,0:T(8,128)} %dynamic-update-slice.13, f32[64,9216]{1,0:T(8,128)} %reshape_reshape.13, s32[]{} %constant.235, s32[]{} %constant.240) | dynamic-update-slice | bytes 4718596
  611.2 28.7 %dynamic-update-slice.18 = f32[64,110736]{1,0:T(8,128)} dynamic-update-slice(f32[64,110736]{1,0:T(8,128)} %dynamic-update-slice.17, f32[64,36864]{1,0:T(8,128)} %reshape_reshape.14, s32[]{} %constant.235, s32[]{} %constant.244) | dynamic-update-slice | bytes 18874372
  641.5 28.3 %dynamic-update-slice.20 = f32[64,110736]{1,0:T(8,128)} dynamic-update-slice(f32[64,110736]{1,0:T(8,128)} %dynamic-update-slice.19, f32[64,36864]{1,0:T(8,128)} %reshape_reshape.15, s32[]{} %constant.235, s32[]{} %constant.246) | dynamic-update-slice | bytes 18874372
  671.3 20.8 %pad.4 = f32[64,111616]{1,0:T(8,128)} pad(f32[64,110736]{1,0:T(8,128)} %dynamic-update-slice.21, f32[]{:T(128)} %constant.53.clone.1), padding=0_0x0_880 | pad | bytes 56922116 | tf_op jit(solution)/shard_map/jit(_pad)/pad | solution.py:27
  692.1 21.0 %reshape.259 = f32[55808,128]{1,0:T(8,128)} reshape(f32[64,111616]{1,0:T(8,128)} %pad.4) | data formatting | bytes 57147392 | tf_op jit(solution)/shard_map/reshape | solution.py:27
  713.8 7.2 add_convert_fusion.1
  721.0 324.2 %reduce-scatter.5.cloned.1.call-done = f32[872,128]{1,0:T(8,128)} async-done(((f32[55808,128]{1,0:T(8,128)}), f32[872,128]{1,0:T(8,128)}) %reduce-scatter.5.cloned.1.call-update) | async-done | bytes 446480
  1047.5 4.4 all-to-all-start
  1051.9 3.1 fusion.20
  1055.0 7.0 all-to-all-done
  (174 shorter events, 71.9 us)
Async XLA Ops:
  7.2 295.3 %copy-start = (s32[128,16]{0,1:T(8,128)S(1)}, s32[128,16]{0,1:T(8,128)}, u32[]{:S(2)}) copy-start(s32[128,16]{0,1:T(8,128)} %param.17) | copy-start | bytes 24580
  7.2 298.9 %all-gather.12.cloned.1.call-start = ((), (), s32[]{:S(2)}) async-start(), calls=%async_computation.4 | async-start | bytes 1597440 | tf_op jit(solution)/shard_map/all_gather | solution.py:82
  7.9 301.3 %all-gather.10.cloned.1.call-start = ((), (), s32[]{:S(2)}) async-start(), calls=%async_computation.3 | async-start | bytes 4792320 | tf_op jit(solution)/shard_map/all_gather | solution.py:82
  8.7 326.6 %all-gather.14.cloned.1.call-start = ((), (), s32[]{:S(2)}) async-start(), calls=%async_computation.5 | async-start | bytes 6389760 | tf_op jit(solution)/shard_map/all_gather | solution.py:82
  9.4 430.7 %all-gather.8.cloned.1.call-start = ((), (), s32[]{:S(2)}) async-start(), calls=%async_computation.2 | async-start | bytes 4792320 | tf_op jit(solution)/shard_map/all_gather | solution.py:82
  10.0 1035.1 %reduce-scatter.5.cloned.1.call-start = ((), (), s32[]{:S(2)}) async-start(), calls=%async_computation.6 | async-start | bytes 29020160
  302.5 13.3 %copy-start.21 = (f32[768]{0:T(1024)}, f32[768]{0:T(1024)S(1)}, u32[]{:S(2)}) copy-start(f32[768]{0:T(1024)S(1)} %convert_element_type.119) | copy-start | bytes 9220
  309.3 6.5 copy-start.3
  321.3 6.4 copy-start.11
  325.1 4.5 copy-start.2
  329.6 3.2 copy-start.14
  335.3 19.9 %copy-start.6 = (f32[512,768]{1,0:T(8,128)S(1)}, f32[512,768]{1,0:T(8,128)}, u32[]{:S(2)}) copy-start(f32[512,768]{1,0:T(8,128)} %copy-done.5) | copy-start | bytes 4718596
  440.1 20.1 %copy-start.9 = (bf16[768,3072]{1,0:T(8,128)(2,1)S(1)}, bf16[768,3072]{1,0:T(8,128)(2,1)}, u32[]{:S(2)}) copy-start(bf16[768,3072]{1,0:T(8,128)(2,1)} %reshape.297) | copy-start | bytes 14155780
  460.2 3.0 copy-start.24
  460.2 3.1 copy-start.7
  460.2 3.1 copy-start.16
  468.6 9.0 copy-start.12
  468.6 9.0 copy-start.13
  468.6 18.5 %slice-start = ((s8[12582912]{0:T(1024)(128)(4,1)}), s8[4194304]{0:T(1024)(128)(4,1)S(1)}, s32[]{:S(2)}) async-start(s8[12582912]{0:T(1024)(128)(4,1)} %bitcast.51), calls=%async_computation.7 | async-start | bytes 8388608
  468.6 18.5 %slice-start.1 = ((s8[12582912]{0:T(1024)(128)(4,1)}), s8[4194304]{0:T(1024)(128)(4,1)S(1)}, s32[]{:S(2)}) async-start(s8[12582912]{0:T(1024)(128)(4,1)} %bitcast.51), calls=%async_computation.8 | async-start | bytes 8388608
  477.5 9.5 slice-start.2
  498.3 4.0 copy-start.22
  507.6 3.1 copy-start.19
  507.6 5.2 copy-start.8
  507.6 5.2 copy-start.25
  507.6 10.9 %slice-start.3 = ((s8[6291456]{0:T(1024)(128)(4,1)}), s8[4194304]{0:T(1024)(128)(4,1)S(1)}, s32[]{:S(2)}) async-start(s8[6291456]{0:T(1024)(128)(4,1)} %bitcast.60), calls=%async_computation.10 | async-start | bytes 8388608
  510.6 7.9 slice-start.5
  512.8 5.7 slice-start.4
  512.8 5.8 slice-start.6
  534.9 11.9 %copy-start.17 = (bf16[512,768]{1,0:T(8,128)(2,1)S(1)}, bf16[512,768]{1,0:T(8,128)(2,1)}, u32[]{:S(2)}) copy-start(bf16[512,768]{1,0:T(8,128)(2,1)} %param.31) | copy-start | bytes 2359300
  1047.5 14.5 %all-to-all-start = ((f32[2,1,110736]{2,1,0:T(1,128)}), f32[2,1,110736]{2,1,0:T(1,128)}, u32[]{:S(2)}, u32[]{:S(2)}) async-start(f32[2,1,110736]{2,1,0:T(1,128)} %broadcast_in_dim.109), calls=%async_computation | async-start | bytes 1773568 | tf_op jit(solution)/shard_map/all_to_all | solution.py:38
  1051.9 16.8 %copy-start.1 = (s32[128,16]{0,1:T(8,128)S(1)}, s32[128,16]{0,1:T(8,128)}, u32[]{:S(2)}) copy-start(s32[128,16]{0,1:T(8,128)} %param.17) | copy-start | bytes 24580
  (7 other events, 11.4 us)
Sparse Core Ops, SparseCore 0:
  9.7 105.3 all-gather.11
  116.8 105.9 all-gather.9
  224.6 108.1 all-gather.13
  334.3 105.7 all-gather.7
  713.2 331.8 reduce-scatter.4
where the time goes:
time: 1090 us; the launch traced here: 1080 us
  waiting for transfers between devices  412 us (38%)
  blocking collectives  282 us (26%)
  local copies, waits for them, and re-layouts  237 us (22%)
  matrix products  96.3 us (9%)
  other arithmetic  27.8 us (3%)
  between operations  15.8 us (1%)
    unnamed x6, waiting for transfers between devices  327 us
    unnamed x1, blocking collectives  282 us
    unnamed x100, local copies, waits for them, and re-layouts  149 us
    all_gather x4, waiting for transfers between devices, fetch(): lax.all_gather(for_sending(params), 'fsdp', axis=0, tiled=True)  78 us
    another operation x4, local copies, waits for them, and re-layouts, sum_packed(): lines = jnp.concatenate([b.reshape(devices, -1) for b in pieces], axis=1)  32.1 us
  transfers between devices with their start and end apart: 6, of which 3 were waited for; matrix products, arithmetic and copies ran while one was open for 7% of the time, Pallas kernels for 0%

commit v1 on v0

v1 whole, which is shorter than its diff:
```python
import functools
import itertools

import jax
import jax.numpy as jnp
from jax import lax
from jax.experimental import pallas as pl
from jax.experimental.pallas import tpu as pltpu
from jax.sharding import PartitionSpec as P

HEADS = 12
HEAD_DIM = 64
LEN = 512
WIDTH = 768
FF = 3072
AXES = ("dp", "fsdp")
F32 = jnp.float32
BF16 = jnp.bfloat16

EVERY = [(y, z, x, c) for y in range(4) for z in range(4) for x in range(4) for c in range(2)]


def index_of(y, z, x, c):
    y, z, x, c = y % 4, z % 4, x % 4, c % 2
    return (y // 2) * 64 + (((y % 2) * 4 + z) * 4 + x) * 2 + c


def moves(by, by_second=None):
    steps = (by, by if by_second is None else by_second)
    return [(index_of(*at), index_of(*(a + s for a, s in zip(at, steps[at[3]])))) for at in EVERY]


Y_RING = moves((1, 0, 0, 0), (-1, 0, 0, 0))
Z_RING = moves((0, 1, 0, 0), (0, -1, 0, 0))
X_RING = moves((0, 0, 1, 0), (0, 0, -1, 0))
Z_BY = {k: moves((0, k, 0, 0)) for k in (1, 2, 3)}
CORES = moves((0, 0, 0, 1))
REPLICA = moves((2, 0, 0, 0))
SPREAD = [
    [
        (index_of(y, z, x, c), index_of(y, z, 2 * (x % 2) + c - k, x // 2))
        for y, z, x, c in EVERY
    ]
    for k in range(4)
]
COLLECT = [[(b, a) for a, b in pairs] for pairs in SPREAD]


def send(array, pairs):
    return lax.ppermute(array, AXES, pairs)


def here():
    at = lax.axis_index("fsdp")
    core, x, z, y = at % 2, (at // 2) % 4, (at // 8) % 4, at // 32
    return y, z, x, core, 1 - 2 * core


def pick(array, at, axis=0):
    return lax.dynamic_index_in_dim(array, at, axis, keepdims=False)


def half_block(shard):
    x = here()[2]
    got = [send(shard, SPREAD[k]) for k in range(4)]
    ring = jnp.stack(got + got[:3])
    return lax.dynamic_slice_in_dim(ring, (4 - x) % 4, 4, 0).reshape(48, shard.shape[1])


def place_pieces(pieces, slots, columns):
    lead = [p.shape[:-2] for p in pieces]
    parts = [
        (n, at) for n, dims in enumerate(lead) for at in itertools.product(*(range(d) for d in dims))
    ]
    count = len(parts)
    starts = [sum(columns[:i]) for i in range(len(columns))]

    def kernel(slots_ref, *refs):
        ins, outs, sem = refs[: len(pieces)], refs[len(pieces) : -1], refs[-1]
        copies = []
        for i, (n, at) in enumerate(parts):
            for o, (start, size) in enumerate(zip(starts, columns)):
                copies.append(
                    pltpu.make_async_copy(
                        ins[n].at[(*at, slice(None), pl.ds(start, size))],
                        outs[o].at[slots_ref[i]],
                        sem.at[i * len(columns) + o],
                    )
                )
        for copy in copies:
            copy.start()
        for copy in copies:
            copy.wait()

    made = pl.pallas_call(
        kernel,
        out_shape=[jax.ShapeDtypeStruct((count, 48, n), BF16) for n in columns],
        in_specs=[pl.BlockSpec(memory_space=pltpu.SMEM)]
        + [pl.BlockSpec(memory_space=pl.ANY)] * len(pieces),
        out_specs=[pl.BlockSpec(memory_space=pl.ANY)] * len(columns),
        scratch_shapes=[pltpu.SemaphoreType.DMA((count * len(columns),))],
        name="place_pieces",
    )(slots, *pieces)
    return [m.reshape(count * 48, n) for m, n in zip(made, columns)]


def gather_rows(shard, columns):
    y, z, x, core, sign = here()
    own, side = [half_block(shard)], []
    for t in range(4):
        if t < 3:
            own.append(send(own[t], Z_RING))
        side.append(send(own[t], Y_RING))
    mine = own + side
    other = [send(p, CORES) for p in mine]
    slots = []
    for half, way in ((core, sign), (1 - core, -sign)):
        for row in (y, 1 - y):
            for t in range(4):
                slots.append((row * 4 + (z - way * t) % 4) * 2 + half)
    return place_pieces(mine + other, jnp.stack(slots), columns)


def gather_back(shard):
    y, z, x, core, sign = here()
    pair = jnp.stack([shard, send(shard, Y_RING)])
    quad = jnp.stack([pair] + [send(pair, Z_BY[k]) for k in (1, 2, 3)])
    mine = [quad]
    for t in range(3):
        mine.append(send(mine[t], X_RING))
    other = [send(p, CORES) for p in mine]
    slots = []
    for half, way in ((core, sign), (1 - core, -sign)):
        for t in range(4):
            for k in range(4):
                for row in (y, 1 - y):
                    at = (row * 4 + (z - k) % 4) * 4 + (x - way * t) % 4
                    slots.append(at * 2 + half)
    return place_pieces(mine + other, jnp.stack(slots), [shard.shape[1]])[0]


def over_replicas(share):
    share = lax.reduce_precision(share, 8, 7)
    return share + send(share.astype(BF16), REPLICA).astype(F32)


def reduce_rows(grad):
    y, z, x, core, sign = here()
    n = grad.shape[1]
    halves = grad.reshape(8, 2, 48, n)
    got = send(pick(halves, 1 - core, 1).astype(BF16), CORES)
    kept = (pick(halves, core, 1) + got.astype(F32)).reshape(2, 4, 48, n)
    mine, theirs = pick(kept, y), pick(kept, 1 - y)
    passed = None
    for t in range(1, 5):
        at = (z - sign * t) % 4
        total = pick(mine, at) + send(pick(theirs, at).astype(BF16), Y_RING).astype(F32)
        if passed is not None:
            total = total + passed.astype(F32)
        if t < 4:
            passed = send(total.astype(BF16), Z_RING)
    pieces = total.astype(BF16).reshape(4, 12, n)
    share = sum(send(pick(pieces, (x + k) % 4), COLLECT[k]).astype(F32) for k in range(4))
    return over_replicas(share)


def reduce_back(grad):
    y, z, x, core, sign = here()
    n = grad.shape[1]
    parts = grad.reshape(2, 4, 4, 2, 48, n)
    got = send(pick(parts, 1 - core, 3).astype(BF16), CORES)
    kept = pick(parts, core, 3) + got.astype(F32)
    passed = None
    for t in range(1, 5):
        total = pick(kept, (x - sign * t) % 4, 2)
        if passed is not None:
            total = total + passed.astype(F32)
        if t < 4:
            passed = send(total.astype(BF16), X_RING)
    low = total.astype(BF16)
    total = pick(total, z, 1) + sum(
        send(pick(low, (z + k) % 4, 1), Z_BY[k]).astype(F32) for k in (1, 2, 3)
    )
    share = pick(total, y) + send(pick(total, 1 - y).astype(BF16), Y_RING).astype(F32)
    return over_replicas(share)


def layer_norm(values, gain, shift):
    centre = values - jnp.mean(values, axis=-1, keepdims=True)
    scale = lax.rsqrt(jnp.mean(centre * centre, axis=-1, keepdims=True) + 1e-05)
    normed = centre * scale
    return (normed * gain + shift, normed, scale)


def norm_back(d_out, normed, scale, gain):
    gain_grad = jnp.sum(d_out * normed, axis=0)
    shift_grad = jnp.sum(d_out, axis=0)
    expand = d_out * gain
    d_in = scale * (
        expand
        - jnp.mean(expand, axis=-1, keepdims=True)
        - normed * jnp.mean(expand * normed, axis=-1, keepdims=True)
    )
    return (d_in, gain_grad, shift_grad)


def dot(a, b, dims):
    return lax.dot_general(a, b, (dims, ((), ())), preferred_element_type=F32)


def attention_probs(query, keys, allowed, logsum):
    scores = jnp.einsum("qhd,khd->hqk", query, keys, preferred_element_type=F32) * HEAD_DIM ** (-0.5)
    scores = jnp.where(allowed[None], scores, -1e30)
    if logsum is None:
        top = jnp.max(scores, axis=-1, keepdims=True)
        logsum = top + jnp.log(jnp.sum(jnp.exp(scores - top), axis=-1, keepdims=True))
    return (jnp.exp(scores - logsum), logsum)


def shards(tokens, lengths, g1, s1, wqkv, qb, vb, wo, ob, g2, s2, w1, bi1, w2, b2, cotangent):
    device = lax.axis_index("dp") * 64 + lax.axis_index("fsdp")
    ends = jnp.cumsum(lax.dynamic_index_in_dim(lengths, device, 0, keepdims=False))
    ids = jnp.sum((ends[None, :] <= jnp.arange(LEN, dtype=jnp.int32)[:, None]).astype(jnp.int32), -1)
    allowed = ids[:, None] == ids[None, :]
    vectors = jnp.stack([g1, s1, qb, vb, ob, g2, s2, b2], axis=1)
    vectors = jnp.concatenate([vectors, bi1.reshape(12, 4)], axis=1)
    vectors = jnp.pad(vectors, ((0, 0), (0, 128 - 12)))
    wqkv, vectors = gather_rows(jnp.concatenate([wqkv, vectors], axis=1), [3 * WIDTH, 128])
    wo, w1 = gather_rows(jnp.concatenate([wo, w1], axis=1), [WIDTH, FF])
    w2 = gather_back(w2)
    rows = vectors.T.astype(F32)
    g1, s1, qb, vb, ob, g2, s2, b2 = (rows[i] for i in range(8))
    bi1 = vectors[:, 8:12].reshape(FF).astype(F32)

    values = tokens.astype(F32)
    normed_out, normed1, scale1 = layer_norm(values, g1, s1)
    act1 = normed_out.astype(BF16)
    bias = jnp.concatenate([qb, jnp.zeros((WIDTH,), F32), vb])
    proj = (dot(act1, wqkv, ((1,), (0,))) + bias).astype(BF16)
    query, keys, vals = (
        proj[:, i * WIDTH : (i + 1) * WIDTH].reshape(LEN, HEADS, HEAD_DIM) for i in range(3)
    )
    probs, logsum = attention_probs(query, keys, allowed, None)
    mixed = (
        jnp.einsum("hqk,khd->qhd", probs.astype(BF16), vals, preferred_element_type=F32)
        .astype(BF16)
        .reshape(LEN, WIDTH)
    )
    middle = values + dot(mixed, wo, ((1,), (0,))) + ob
    normed_out2, normed2, scale2 = layer_norm(middle, g2, s2)
    act2 = normed_out2.astype(BF16)
    pre = dot(act2, w1, ((1,), (0,))) + bi1
    gact = jax.nn.gelu(pre, approximate=False).astype(BF16)
    result = middle + dot(gact, w2, ((1,), (0,))) + b2

    d_up = cotangent
    grad_w2 = dot(gact, d_up, ((0,), (0,)))
    back_share = reduce_back(grad_w2)
    grad_b2 = jnp.sum(d_up.astype(F32), axis=0)
    d_gact = dot(d_up, w2, ((1,), (1,)))
    d_pre = jax.vjp(lambda a: jax.nn.gelu(a, approximate=False), pre)[1](d_gact)[0].astype(BF16)
    grad_bi1 = jnp.sum(d_pre.astype(F32), axis=0)
    grad_w1 = dot(act2, d_pre, ((0,), (0,)))
    in_share = reduce_rows(grad_w1)
    d_act2 = dot(d_pre, w1, ((1,), (1,)))
    d_mid_ln, grad_g2, grad_s2 = norm_back(d_act2, normed2, scale2, g2)
    d_middle = cotangent.astype(F32) + d_mid_ln
    d_branch = d_middle.astype(BF16)
    grad_wo = dot(mixed, d_branch, ((0,), (0,)))
    grad_ob = jnp.sum(d_branch.astype(F32), axis=0)
    d_mixed = dot(d_branch, wo, ((1,), (1,))).astype(BF16).reshape(LEN, HEADS, HEAD_DIM)

    probs, unused = attention_probs(query, keys, allowed, logsum)
    d_probs = jnp.einsum("qhd,khd->hqk", d_mixed, vals, preferred_element_type=F32)
    d_scores = (probs * (d_probs - jnp.sum(probs * d_probs, axis=-1, keepdims=True))).astype(BF16)
    scale = HEAD_DIM ** (-0.5)
    d_query = jnp.einsum("hqk,khd->qhd", d_scores, keys, preferred_element_type=F32) * scale
    d_keys = jnp.einsum("hqk,qhd->khd", d_scores, query, preferred_element_type=F32) * scale
    d_vals = jnp.einsum("hqk,qhd->khd", probs.astype(BF16), d_mixed, preferred_element_type=F32)
    d_proj = jnp.concatenate(
        [d.reshape(LEN, WIDTH) for d in (d_query, d_keys, d_vals)], axis=1
    ).astype(BF16)
    grad_qb = jnp.sum(d_proj[:, :WIDTH].astype(F32), axis=0)
    grad_vb = jnp.sum(d_proj[:, 2 * WIDTH :].astype(F32), axis=0)
    grad_wqkv = dot(act1, d_proj, ((0,), (0,)))
    d_act1 = dot(d_proj, wqkv, ((1,), (1,)))
    d_in_ln, grad_g1, grad_s1 = norm_back(d_act1, normed1, scale1, g1)
    d_input = d_middle + d_in_ln
    columns = jnp.stack([grad_g1, grad_s1, grad_qb, grad_vb, grad_ob, grad_g2, grad_s2, grad_b2], 1)
    columns = jnp.concatenate([columns, grad_bi1.reshape(WIDTH, 4)], axis=1)
    columns = jnp.pad(columns, ((0, 0), (0, 128 - 12)))
    rest = reduce_rows(jnp.concatenate([grad_wqkv, grad_wo, columns], axis=1))
    own = rest[:, 4 * WIDTH :]
    return (
        result.astype(BF16),
        d_input,
        own[:, 0],
        own[:, 1],
        rest[:, : 3 * WIDTH],
        own[:, 2],
        own[:, 3],
        rest[:, 3 * WIDTH : 4 * WIDTH],
        own[:, 4],
        own[:, 5],
        own[:, 6],
        in_share,
        own[:, 8:12].reshape(48),
        back_share,
        own[:, 7],
    )


def solution(mesh):
    rows, whole = P(AXES, None), P()
    vector, matrix = P("fsdp"), P("fsdp", None)
    weights = (
        vector, vector, matrix, vector, vector, matrix, vector,
        vector, vector, matrix, vector, matrix, vector,
    )
    return jax.shard_map(
        shards,
        mesh=mesh,
        in_specs=(rows, whole, *weights, rows),
        out_specs=(rows, rows, *weights),
        check_vma=False,
    )
```

time: 1090 us -> 815 us (0.75)
  Pallas kernels: 0 us -> 441 us
  waiting for transfers between devices: 412 us -> 93.9 us
  blocking collectives: 282 us -> 0 us
  local copies, waits for them, and re-layouts: 237 us -> 49.2 us
  starting transfers between devices: 4.55 us -> 84.6 us
  between operations: 15.8 us -> 3.13 us
    pallas_call x0 -> x3, Pallas kernels: none -> 441 us  [place_pieces(): pl.pallas_call(kernel, out_shape=[jax.ShapeDtypeStruct((count, 48, n), BF...]
    unnamed x6 -> x0, waiting for transfers between devices: 327 us -> none
    unnamed x1 -> x0, blocking collectives: 282 us -> none
    unnamed x100 -> x123, local copies, waits for them, and re-layouts: 149 us -> 8.34 us
    ppermute x0 -> x84, waiting for transfers between devices: none -> 93.9 us  [send(): return lax.ppermute(array, AXES, pairs)]
    ppermute x0 -> x84, starting transfers between devices: none -> 84.6 us  [send(): return lax.ppermute(array, AXES, pairs)]
    all_gather x4 -> x0, waiting for transfers between devices: 78 us -> none  [fetch(): lax.all_gather(for_sending(params), 'fsdp', axis=0, tiled=True)]
    pad x1 -> x0, local copies, waits for them, and re-layouts: 20.8 us -> none  [sum_packed(): jnp.pad(lines, ((0, 0), (0, extent * 128 - lines.shape[1])))]
  transfers between devices with their start and end apart: 6 -> 84, of which waited for: 3 -> 25; matrix products, arithmetic and copies ran while one was open for 7% -> 20% of each run, Pallas kernels for 0% -> 55%
where the time goes in v1:
time: 815 us; the launch traced here: 805 us
  Pallas kernels  441 us (54%)
  matrix products  96.5 us (12%)
  waiting for transfers between devices  93.9 us (12%)
  starting transfers between devices  84.6 us (10%)
  local copies, waits for them, and re-layouts  49.2 us (6%)
  other arithmetic  36.3 us (4%)
    pallas_call x3, Pallas kernels, place_pieces(): pl.pallas_call(kernel, out_shape=[jax.ShapeDtypeStruct((count, 48, n), BF...  441 us
    ppermute x84, waiting for transfers between devices, send(): return lax.ppermute(array, AXES, pairs)  93.9 us
    ppermute x84, starting transfers between devices, send(): return lax.ppermute(array, AXES, pairs)  84.6 us
    dot_general x12, matrix products, dot(): return lax.dot_general(a, b, (dims, ((), ())), preferred_element_type=F32)  64.5 us
  transfers between devices with their start and end apart: 84, of which 25 were waited for; matrix products, arithmetic and copies ran while one was open for 20% of the time, Pallas kernels for 55%

profile of v1, /device:TPU:0, one launch (start us, length us, event | category | flops | bytes accessed | tf_op | source)
XLA Modules:
  0.0 805.0 jit_solution(13988255211990777857)
XLA Ops:
  8.5 3.5 collective-permute-start.3
  13.7 4.8 collective-permute-start.1
  26.1 3.6 collective-permute-start.21
  35.7 4.0 collective-permute-done.38
  43.2 3.6 collective-permute-start.40
  80.4 115.2 %place_pieces.3 = (bf16[16,48,2304]{2,1,0:T(8,128)(2,1)}, bf16[16,48,128]{2,1,0:T(8,128)(2,1)}) custom-call(s32[16]{0:T(128)} %stack.387.slots_ref, bf16[48,2432]{1,0:T(8,128)(2,1)} %copy-done.15, bf16[48,2432]{1,0:T(8,128)(2,1)} %copy-done.21, bf16[48,2432]{1,0:T(8,128)(2,1)} %collective-permute-done.5.refs_2_, bf16[48,2432]{1,0:T(8,128)(2,1)} %copy-done.25, ...), custom_call_target="tpu_custom_call" | custom-call | tf_op jit(solution)/shard_map/place_pieces/pallas_call | solution.py:95
  197.4 4.2 fusion.15
  219.1 8.7 %convolution_convert_fusion.2 = bf16[12,64,512]{2,1,0:T(8,128)(2,1)} fusion(bf16[512,12,64]{0,2,1:T(8,128)(2,1)S(1)} %bitcast.343, f32[12,512,512]{1,2,0:T(8,128)} %copy-done.2, f32[12,512]{1,0:T(8,128)S(1)} %log_add_fusion, pred[512,512]{0,1:T(8,128)(4,1)S(1)} %broadcast_compare_fusion), kind=kOutput, calls=%fused_computation.80 | convolution fusion | flops 415629312 | bytes 14442496 | tf_op jit(solution)/shard_map/hqk,khd->qhd/dot_general | solution.py:245
  232.4 180.7 %place_pieces.4 = (bf16[16,48,768]{2,1,0:T(8,128)(2,1)}, bf16[16,48,3072]{2,1,0:T(8,128)(2,1)}) custom-call(s32[16]{0:T(128)} %stack.387.slots_ref, bf16[48,3840]{1,0:T(8,128)(2,1)} %reshape.273.refs_0_, bf16[48,3840]{1,0:T(8,128)(2,1)} %collective-permute-done.23.refs_1_, bf16[48,3840]{1,0:T(8,128)(2,1)} %collective-permute-done.24.refs_2_, ...), custom_call_target="tpu_custom_call" | custom-call | tf_op jit(solution)/shard_map/place_pieces/pallas_call | solution.py:95
  415.9 18.4 %multiply_convert_fusion.1 = (bf16[512,3072]{1,0:T(8,128)(2,1)S(1)}, f32[512,3072]{1,0:T(8,128)}, f32[512,3072]{1,0:T(8,128)}) fusion(f32[3072]{0:T(1024)S(1)} %reshape.290, bf16[768,3072]{1,0:T(8,128)(2,1)S(1)} %bitcast.369, f32[512,768]{1,0:T(8,128)S(1)} %get-tuple-element.81, f32[768]{0:T(1024)S(1)} %get-tuple-element.32, ...), kind=kOutput, calls=%fused_computation.21 | convolution fusion | flops 2521694208 | bytes 22042624 | tf_op jit(solution)/shard_map/dot_general | solution.py:208
  437.4 3.5 copy-done.9
  444.0 145.3 %place_pieces.5 = bf16[64,48,768]{2,1,0:T(8,128)(2,1)} custom-call(s32[64]{0:T(128)} %stack.470.slots_ref, bf16[4,2,48,768]{3,2,1,0:T(8,128)(2,1)} %pad_maximum_fusion.3.refs_0_, bf16[4,2,48,768]{3,2,1,0:T(8,128)(2,1)} %collective-permute-done.42.refs_1_, bf16[4,2,48,768]{3,2,1,0:T(8,128)(2,1)} %collective-permute-done.43.refs_2_, ...), custom_call_target="tpu_custom_call" | custom-call | tf_op jit(solution)/shard_map/place_pieces/pallas_call | solution.py:95
  589.3 8.7 %convert_reduce_fusion = (f32[3072]{0:T(1024)S(1)}, bf16[512,3072]{1,0:T(8,128)(2,1)S(1)}) fusion(f32[512,3072]{1,0:T(8,128)} %get-tuple-element.52, bf16[3072,768]{1,0:T(8,128)(2,1)} %bitcast.339, bf16[512,768]{1,0:T(8,128)(2,1)S(1)} %copy-done.16, f32[512,3072]{1,0:T(8,128)} %get-tuple-element.82, f32[3072]{0:T(1024)S(1)} %reshape.290), kind=kOutput, calls=%fused_computation.20 | convolution fusion | flops 2442654720 | bytes 21258240 | tf_op jit(solution)/shard_map/dot_general | solution.py:208
  598.0 6.0 multiply_reduce_fusion.1
  604.0 5.5 fusion.83
  614.8 8.1 %convolution_convert_fusion.1 = bf16[12,64,512]{2,1,0:T(8,128)(2,1)S(1)} fusion(bf16[512,12,64]{0,2,1:T(8,128)(2,1)} %bitcast.345, f32[12,512,512]{1,2,0:T(8,128)} %copy-done.2, f32[12,512]{1,0:T(8,128)S(1)} %log_add_fusion, pred[512,512]{0,1:T(8,128)(4,1)S(1)} %broadcast_compare_fusion), kind=kOutput, calls=%fused_computation.79 | convolution fusion | flops 415629312 | bytes 14442496 | tf_op jit(solution)/shard_map/hqk,qhd->khd/dot_general | solution.py:279
  622.9 10.0 %multiply_reduce_fusion = (f32[12,512]{1,0:T(8,128)S(1)}, f32[12,512,512]{1,2,0:T(8,128)}) fusion(f32[12,512,512]{1,2,0:T(8,128)} %copy-done.2, f32[12,512]{1,0:T(8,128)S(1)} %log_add_fusion, pred[512,512]{0,1:T(8,128)(4,1)S(1)} %broadcast_compare_fusion, bf16[512,12,64]{0,2,1:T(8,128)(2,1)S(1)} %bitcast.346, bf16[512,12,64]{0,2,1:T(8,128)(2,1)S(1)} %bitcast.344), kind=kOutput, calls=%fused_computation.1 | convolution fusion | flops 418375680 | bytes 27049984 | tf_op jit(solution)/shard_map/qhd,khd->hqk/dot_general | solution.py:274
  633.0 6.8 multiply_convert_fusion
  643.5 4.2 fusion.31
  647.7 5.2 fusion.36
  657.8 4.1 fusion.17
  677.3 3.5 add_convert_fusion
  685.4 9.2 %collective-permute-done.76 = bf16[2,4,48,768]{3,2,1,0:T(8,128)(2,1)S(1)} collective-permute-done((bf16[2,4,48,768]{3,2,1,0:T(8,128)(2,1)S(1)}, bf16[2,4,48,768]{3,2,1,0:T(8,128)(2,1)S(1)}, u32[]{:S(2)}, u32[]{:S(2)}) %collective-permute-start.76) | collective-permute-done | bytes 589856 | tf_op jit(solution)/shard_map/ppermute | solution.py:50
  694.9 3.7 bitcast_add_fusion.2
  705.8 4.1 collective-permute-done.66
  710.0 9.5 %collective-permute-done.53 = bf16[48,3200]{1,0:T(8,128)(2,1)S(1)} collective-permute-done((bf16[48,3200]{1,0:T(8,128)(2,1)S(1)}, bf16[48,3200]{1,0:T(8,128)(2,1)S(1)}, u32[]{:S(2)}, u32[]{:S(2)}) %collective-permute-start.53) | collective-permute-done | bytes 307232 | tf_op jit(solution)/shard_map/ppermute | solution.py:50
  722.3 5.1 collective-permute-done.67
  727.8 4.7 collective-permute-done.52
  736.3 7.3 collective-permute-done.68
  743.8 7.9 collective-permute-done.55
  759.8 4.5 collective-permute-start.71
  770.2 8.6 %collective-permute-done.79 = bf16[2,48,768]{2,1,0:T(8,128)(2,1)S(1)} collective-permute-done((bf16[2,48,768]{2,1,0:T(8,128)(2,1)S(1)}, bf16[2,48,768]{2,1,0:T(8,128)(2,1)S(1)}, u32[]{:S(2)}, u32[]{:S(2)}) %collective-permute-start.79) | collective-permute-done | bytes 147488 | tf_op jit(solution)/shard_map/ppermute | solution.py:50
  (388 shorter events, 179.6 us)
Async XLA Ops:
  8.5 25.3 %collective-permute-start.3 = (bf16[12,2432]{1,0:T(8,128)(2,1)S(1)}, bf16[12,2432]{1,0:T(8,128)(2,1)S(1)}, u32[]{:S(2)}, u32[]{:S(2)}) collective-permute-start(bf16[12,2432]{1,0:T(8,128)(2,1)S(1)} %fusion.64), channel_id=1, source_target_pairs={{0,2},{1,4},{2,6},{3,0},{4,3},{5,5},{6,7},{7,1},{8,10},{9,12},{10,... | collective-permute-start | bytes 175112 | tf_op jit(solution)/shard_map/ppermute | solution.py:50
  12.0 20.2 %collective-permute-start.2 = (bf16[12,2432]{1,0:T(8,128)(2,1)S(1)}, bf16[12,2432]{1,0:T(8,128)(2,1)S(1)}, u32[]{:S(2)}, u32[]{:S(2)}) collective-permute-start(bf16[12,2432]{1,0:T(8,128)(2,1)S(1)} %fusion.64), channel_id=1, source_target_pairs={{0,4},{1,6},{2,0},{3,2},{4,5},{5,7},{6,1},{7,3},{8,12},{9,14},{10,... | collective-permute-start | bytes 175112 | tf_op jit(solution)/shard_map/ppermute | solution.py:50
  13.7 16.1 %collective-permute-start.1 = (bf16[12,2432]{1,0:T(8,128)(2,1)S(1)}, bf16[12,2432]{1,0:T(8,128)(2,1)S(1)}, u32[]{:S(2)}, u32[]{:S(2)}) collective-permute-start(bf16[12,2432]{1,0:T(8,128)(2,1)S(1)} %fusion.64), channel_id=1, source_target_pairs={{0,6},{1,0},{2,2},{3,4},{4,7},{5,1},{6,3},{7,5},{8,14},{9,8},{10,1... | collective-permute-start | bytes 175112 | tf_op jit(solution)/shard_map/ppermute | solution.py:50
  22.1 28.1 %collective-permute-start.22 = (bf16[12,3840]{1,0:T(8,128)(2,1)}, bf16[12,3840]{1,0:T(8,128)(2,1)S(1)}, u32[]{:S(2)}, u32[]{:S(2)}) collective-permute-start(bf16[12,3840]{1,0:T(8,128)(2,1)} %constant_dynamic-update-slice_fusion), channel_id=1, source_target_pairs={{0,2},{1,4},{2,6},{3,0},{4,3},{5,5},{6,7},{7,1},{8,10},{9,12},{10,... | collective-permute-start | bytes 276488 | tf_op jit(solution)/shard_map/ppermute | solution.py:50
  26.1 20.8 %collective-permute-start.21 = (bf16[12,3840]{1,0:T(8,128)(2,1)}, bf16[12,3840]{1,0:T(8,128)(2,1)S(1)}, u32[]{:S(2)}, u32[]{:S(2)}) collective-permute-start(bf16[12,3840]{1,0:T(8,128)(2,1)} %constant_dynamic-update-slice_fusion), channel_id=1, source_target_pairs={{0,4},{1,6},{2,0},{3,2},{4,5},{5,7},{6,1},{7,3},{8,12},{9,14},{10,... | collective-permute-start | bytes 276488 | tf_op jit(solution)/shard_map/ppermute | solution.py:50
  29.7 17.0 %collective-permute-start.20 = (bf16[12,3840]{1,0:T(8,128)(2,1)}, bf16[12,3840]{1,0:T(8,128)(2,1)S(1)}, u32[]{:S(2)}, u32[]{:S(2)}) collective-permute-start(bf16[12,3840]{1,0:T(8,128)(2,1)} %constant_dynamic-update-slice_fusion), channel_id=1, source_target_pairs={{0,6},{1,0},{2,2},{3,4},{4,7},{5,1},{6,3},{7,5},{8,14},{9,8},{10,1... | collective-permute-start | bytes 276488 | tf_op jit(solution)/shard_map/ppermute | solution.py:50
  76.7 128.6 %collective-permute-start.30 = (bf16[48,3840]{1,0:T(8,128)(2,1)}, bf16[48,3840]{1,0:T(8,128)(2,1)}, u32[]{:S(2)}, u32[]{:S(2)}) collective-permute-start(bf16[48,3840]{1,0:T(8,128)(2,1)} %reshape.273.refs_0_), channel_id=1, source_target_pairs={{0,1},{1,0},{2,3},{3,2},{4,5},{5,4},{6,7},{7,6},{8,9},{9,8},{10,11... | collective-permute-start | bytes 1105928 | tf_op jit(solution)/shard_map/ppermute | solution.py:50
  76.7 128.7 %collective-permute-start.26 = (bf16[48,3840]{1,0:T(8,128)(2,1)}, bf16[48,3840]{1,0:T(8,128)(2,1)}, u32[]{:S(2)}, u32[]{:S(2)}) collective-permute-start(bf16[48,3840]{1,0:T(8,128)(2,1)} %reshape.273.refs_0_), channel_id=1, source_target_pairs={{0,32},{1,97},{2,34},{3,99},{4,36},{5,101},{6,38},{7,103},{8,40},{... | collective-permute-start | bytes 1105928 | tf_op jit(solution)/shard_map/ppermute | solution.py:50
  76.8 129.1 %collective-permute-start.42 = (bf16[4,2,48,768]{3,2,1,0:T(8,128)(2,1)}, bf16[4,2,48,768]{3,2,1,0:T(8,128)(2,1)}, u32[]{:S(2)}, u32[]{:S(2)}) collective-permute-start(bf16[4,2,48,768]{3,2,1,0:T(8,128)(2,1)} %pad_maximum_fusion.3.refs_0_), channel_id=1, source_target_pairs={{0,2},{1,7},{2,4},{3,1},{4,6},{5,3},{6,0},{7,5},{8,10},{9,15},{10,... | collective-permute-start | bytes 1769480 | tf_op jit(solution)/shard_map/ppermute | solution.py:50
  78.4 128.5 %collective-permute-start.27 = (bf16[48,3840]{1,0:T(8,128)(2,1)}, bf16[48,3840]{1,0:T(8,128)(2,1)}, u32[]{:S(2)}, u32[]{:S(2)}) collective-permute-start(bf16[48,3840]{1,0:T(8,128)(2,1)} %collective-permute-done.23.refs_1_), channel_id=1, source_target_pairs={{0,32},{1,97},{2,34},{3,99},{4,36},{5,101},{6,38},{7,103},{8,40},{... | collective-permute-start | bytes 1105928 | tf_op jit(solution)/shard_map/ppermute | solution.py:50
  80.3 127.2 %collective-permute-start.25 = (bf16[48,3840]{1,0:T(8,128)(2,1)}, bf16[48,3840]{1,0:T(8,128)(2,1)}, u32[]{:S(2)}, u32[]{:S(2)}) collective-permute-start(bf16[48,3840]{1,0:T(8,128)(2,1)} %collective-permute-done.24.refs_2_), channel_id=1, source_target_pairs={{0,8},{1,25},{2,10},{3,27},{4,12},{5,29},{6,14},{7,31},{8,16},{9,1... | collective-permute-start | bytes 1105928 | tf_op jit(solution)/shard_map/ppermute | solution.py:50
  213.1 17.3 %collective-permute-start.43 = (bf16[4,2,48,768]{3,2,1,0:T(8,128)(2,1)}, bf16[4,2,48,768]{3,2,1,0:T(8,128)(2,1)}, u32[]{:S(2)}, u32[]{:S(2)}) collective-permute-start(bf16[4,2,48,768]{3,2,1,0:T(8,128)(2,1)} %collective-permute-done.42.refs_1_), channel_id=1, source_target_pairs={{0,2},{1,7},{2,4},{3,1},{4,6},{5,3},{6,0},{7,5},{8,10},{9,15},{10,... | collective-permute-start | bytes 1769480 | tf_op jit(solution)/shard_map/ppermute | solution.py:50
  215.6 14.3 %collective-permute-start.32 = (bf16[48,3840]{1,0:T(8,128)(2,1)}, bf16[48,3840]{1,0:T(8,128)(2,1)}, u32[]{:S(2)}, u32[]{:S(2)}) collective-permute-start(bf16[48,3840]{1,0:T(8,128)(2,1)} %collective-permute-done.24.refs_2_), channel_id=1, source_target_pairs={{0,1},{1,0},{2,3},{3,2},{4,5},{5,4},{6,7},{7,6},{8,9},{9,8},{10,11... | collective-permute-start | bytes 1105928 | tf_op jit(solution)/shard_map/ppermute | solution.py:50
  215.6 15.4 %collective-permute-start.33 = (bf16[48,3840]{1,0:T(8,128)(2,1)}, bf16[48,3840]{1,0:T(8,128)(2,1)}, u32[]{:S(2)}, u32[]{:S(2)}) collective-permute-start(bf16[48,3840]{1,0:T(8,128)(2,1)} %collective-permute-done.25.refs_3_), channel_id=1, source_target_pairs={{0,1},{1,0},{2,3},{3,2},{4,5},{5,4},{6,7},{7,6},{8,9},{9,8},{10,11... | collective-permute-start | bytes 1105928 | tf_op jit(solution)/shard_map/ppermute | solution.py:50
  216.1 14.4 %collective-permute-start.36 = (bf16[48,3840]{1,0:T(8,128)(2,1)}, bf16[48,3840]{1,0:T(8,128)(2,1)}, u32[]{:S(2)}, u32[]{:S(2)}) collective-permute-start(bf16[48,3840]{1,0:T(8,128)(2,1)} %collective-permute-done.28.refs_6_), channel_id=1, source_target_pairs={{0,1},{1,0},{2,3},{3,2},{4,5},{5,4},{6,7},{7,6},{8,9},{9,8},{10,11... | collective-permute-start | bytes 1105928 | tf_op jit(solution)/shard_map/ppermute | solution.py:50
  218.9 13.5 %collective-permute-start.37 = (bf16[48,3840]{1,0:T(8,128)(2,1)}, bf16[48,3840]{1,0:T(8,128)(2,1)}, u32[]{:S(2)}, u32[]{:S(2)}) collective-permute-start(bf16[48,3840]{1,0:T(8,128)(2,1)} %collective-permute-done.29.refs_7_), channel_id=1, source_target_pairs={{0,1},{1,0},{2,3},{3,2},{4,5},{5,4},{6,7},{7,6},{8,9},{9,8},{10,11... | collective-permute-start | bytes 1105928 | tf_op jit(solution)/shard_map/ppermute | solution.py:50
  229.9 213.2 %collective-permute-start.45 = (bf16[4,2,48,768]{3,2,1,0:T(8,128)(2,1)}, bf16[4,2,48,768]{3,2,1,0:T(8,128)(2,1)}, u32[]{:S(2)}, u32[]{:S(2)}) collective-permute-start(bf16[4,2,48,768]{3,2,1,0:T(8,128)(2,1)} %pad_maximum_fusion.3.refs_0_), channel_id=1, source_target_pairs={{0,1},{1,0},{2,3},{3,2},{4,5},{5,4},{6,7},{7,6},{8,9},{9,8},{10,11... | collective-permute-start | bytes 1769480 | tf_op jit(solution)/shard_map/ppermute | solution.py:50
  230.5 212.7 %collective-permute-start.46 = (bf16[4,2,48,768]{3,2,1,0:T(8,128)(2,1)}, bf16[4,2,48,768]{3,2,1,0:T(8,128)(2,1)}, u32[]{:S(2)}, u32[]{:S(2)}) collective-permute-start(bf16[4,2,48,768]{3,2,1,0:T(8,128)(2,1)} %collective-permute-done.42.refs_1_), channel_id=1, source_target_pairs={{0,1},{1,0},{2,3},{3,2},{4,5},{5,4},{6,7},{7,6},{8,9},{9,8},{10,11... | collective-permute-start | bytes 1769480 | tf_op jit(solution)/shard_map/ppermute | solution.py:50
  230.6 212.6 %collective-permute-start.47 = (bf16[4,2,48,768]{3,2,1,0:T(8,128)(2,1)}, bf16[4,2,48,768]{3,2,1,0:T(8,128)(2,1)}, u32[]{:S(2)}, u32[]{:S(2)}) collective-permute-start(bf16[4,2,48,768]{3,2,1,0:T(8,128)(2,1)} %collective-permute-done.43.refs_2_), channel_id=1, source_target_pairs={{0,1},{1,0},{2,3},{3,2},{4,5},{5,4},{6,7},{7,6},{8,9},{9,8},{10,11... | collective-permute-start | bytes 1769480 | tf_op jit(solution)/shard_map/ppermute | solution.py:50
  231.0 203.3 %collective-permute-start.44 = (bf16[4,2,48,768]{3,2,1,0:T(8,128)(2,1)}, bf16[4,2,48,768]{3,2,1,0:T(8,128)(2,1)}, u32[]{:S(2)}, u32[]{:S(2)}) collective-permute-start(bf16[4,2,48,768]{3,2,1,0:T(8,128)(2,1)} %collective-permute-done.43.refs_2_), channel_id=1, source_target_pairs={{0,2},{1,7},{2,4},{3,1},{4,6},{5,3},{6,0},{7,5},{8,10},{9,15},{10,... | collective-permute-start | bytes 1769480 | tf_op jit(solution)/shard_map/ppermute | solution.py:50
  442.7 238.2 %collective-permute-start.75 = (bf16[2,4,4,48,768]{4,3,2,1,0:T(8,128)(2,1)}, bf16[2,4,4,48,768]{4,3,2,1,0:T(8,128)(2,1)}, u32[]{:S(2)}, u32[]{:S(2)}) collective-permute-start(bf16[2,4,4,48,768]{4,3,2,1,0:T(8,128)(2,1)} %fusion.18), channel_id=1, source_target_pairs={{0,1},{1,0},{2,3},{3,2},{4,5},{5,4},{6,7},{7,6},{8,9},{9,8},{10,11... | collective-permute-start | bytes 7077896 | tf_op jit(solution)/shard_map/ppermute | solution.py:50
  661.8 33.0 %collective-permute-start.62 = (bf16[8,48,3072]{2,1,0:T(8,128)(2,1)}, bf16[8,48,3072]{2,1,0:T(8,128)(2,1)}, u32[]{:S(2)}, u32[]{:S(2)}) collective-permute-start(bf16[8,48,3072]{2,1,0:T(8,128)(2,1)} %fusion.17), channel_id=1, source_target_pairs={{0,1},{1,0},{2,3},{3,2},{4,5},{5,4},{6,7},{7,6},{8,9},{9,8},{10,11... | collective-permute-start | bytes 7077896 | tf_op jit(solution)/shard_map/ppermute | solution.py:50
  675.2 26.3 %collective-permute-start.49 = (bf16[8,48,3200]{2,1,0:T(8,128)(2,1)S(1)}, bf16[8,48,3200]{2,1,0:T(8,128)(2,1)}, u32[]{:S(2)}, u32[]{:S(2)}) collective-permute-start(bf16[8,48,3200]{2,1,0:T(8,128)(2,1)S(1)} %fusion.16), channel_id=1, source_target_pairs={{0,1},{1,0},{2,3},{3,2},{4,5},{5,4},{6,7},{7,6},{8,9},{9,8},{10,11... | collective-permute-start | bytes 7372808 | tf_op jit(solution)/shard_map/ppermute | solution.py:50
  694.8 26.3 %collective-permute-start.77 = (bf16[2,4,48,768]{3,2,1,0:T(8,128)(2,1)S(1)}, bf16[2,4,48,768]{3,2,1,0:T(8,128)(2,1)S(1)}, u32[]{:S(2)}, u32[]{:S(2)}) collective-permute-start(bf16[2,4,48,768]{3,2,1,0:T(8,128)(2,1)S(1)} %fusion.34), channel_id=1, source_target_pairs={{0,2},{1,7},{2,4},{3,1},{4,6},{5,3},{6,0},{7,5},{8,10},{9,15},{10,... | collective-permute-start | bytes 1769480 | tf_op jit(solution)/shard_map/ppermute | solution.py:50
  698.7 53.3 %collective-permute-start.63 = (bf16[48,3072]{1,0:T(8,128)(2,1)S(1)}, bf16[48,3072]{1,0:T(8,128)(2,1)S(1)}, u32[]{:S(2)}, u32[]{:S(2)}) collective-permute-start(bf16[48,3072]{1,0:T(8,128)(2,1)S(1)} %get-tuple-element.57), channel_id=1, source_target_pairs={{0,32},{1,97},{2,34},{3,99},{4,36},{5,101},{6,38},{7,103},{8,40},{... | collective-permute-start | bytes 884744 | tf_op jit(solution)/shard_map/ppermute | solution.py:50
  701.4 19.8 %collective-permute-start.65 = (bf16[48,3072]{1,0:T(8,128)(2,1)S(1)}, bf16[48,3072]{1,0:T(8,128)(2,1)S(1)}, u32[]{:S(2)}, u32[]{:S(2)}) collective-permute-start(bf16[48,3072]{1,0:T(8,128)(2,1)S(1)} %get-tuple-element.59), channel_id=1, source_target_pairs={{0,32},{1,97},{2,34},{3,99},{4,36},{5,101},{6,38},{7,103},{8,40},{... | collective-permute-start | bytes 884744 | tf_op jit(solution)/shard_map/ppermute | solution.py:50
  701.5 34.3 %collective-permute-start.64 = (bf16[48,3072]{1,0:T(8,128)(2,1)S(1)}, bf16[48,3072]{1,0:T(8,128)(2,1)S(1)}, u32[]{:S(2)}, u32[]{:S(2)}) collective-permute-start(bf16[48,3072]{1,0:T(8,128)(2,1)S(1)} %get-tuple-element.60), channel_id=1, source_target_pairs={{0,32},{1,97},{2,34},{3,99},{4,36},{5,101},{6,38},{7,103},{8,40},{... | collective-permute-start | bytes 884744 | tf_op jit(solution)/shard_map/ppermute | solution.py:50
  721.0 59.4 %collective-permute-start.50 = (bf16[48,3200]{1,0:T(8,128)(2,1)S(1)}, bf16[48,3200]{1,0:T(8,128)(2,1)S(1)}, u32[]{:S(2)}, u32[]{:S(2)}) collective-permute-start(bf16[48,3200]{1,0:T(8,128)(2,1)S(1)} %get-tuple-element.53), channel_id=1, source_target_pairs={{0,32},{1,97},{2,34},{3,99},{4,36},{5,101},{6,38},{7,103},{8,40},{... | collective-permute-start | bytes 921608 | tf_op jit(solution)/shard_map/ppermute | solution.py:50
  735.8 16.0 %collective-permute-start.78 = (bf16[2,4,48,768]{3,2,1,0:T(8,128)(2,1)S(1)}, bf16[2,4,48,768]{3,2,1,0:T(8,128)(2,1)S(1)}, u32[]{:S(2)}, u32[]{:S(2)}) collective-permute-start(bf16[2,4,48,768]{3,2,1,0:T(8,128)(2,1)S(1)} %fusion.35), channel_id=1, source_target_pairs={{0,2},{1,7},{2,4},{3,1},{4,6},{5,3},{6,0},{7,5},{8,10},{9,15},{10,... | collective-permute-start | bytes 1769480 | tf_op jit(solution)/shard_map/ppermute | solution.py:50
  764.3 16.2 %collective-permute-start.56 = (bf16[48,3200]{1,0:T(8,128)(2,1)S(1)}, bf16[48,3200]{1,0:T(8,128)(2,1)S(1)}, u32[]{:S(2)}, u32[]{:S(2)}) collective-permute-start(bf16[48,3200]{1,0:T(8,128)(2,1)S(1)} %fusion.42), channel_id=1, source_target_pairs={{0,8},{1,25},{2,10},{3,27},{4,12},{5,29},{6,14},{7,31},{8,16},{9,1... | collective-permute-start | bytes 921608 | tf_op jit(solution)/shard_map/ppermute | solution.py:50
  764.4 14.4 %collective-permute-start.79 = (bf16[2,48,768]{2,1,0:T(8,128)(2,1)S(1)}, bf16[2,48,768]{2,1,0:T(8,128)(2,1)S(1)}, u32[]{:S(2)}, u32[]{:S(2)}) collective-permute-start(bf16[2,48,768]{2,1,0:T(8,128)(2,1)S(1)} %get-tuple-element.65), channel_id=1, source_target_pairs={{0,8},{1,9},{2,10},{3,11},{4,12},{5,13},{6,14},{7,15},{8,16},{9,17... | collective-permute-start | bytes 442376 | tf_op jit(solution)/shard_map/ppermute | solution.py:50
  767.9 12.4 %collective-permute-start.81 = (bf16[2,48,768]{2,1,0:T(8,128)(2,1)S(1)}, bf16[2,48,768]{2,1,0:T(8,128)(2,1)S(1)}, u32[]{:S(2)}, u32[]{:S(2)}) collective-permute-start(bf16[2,48,768]{2,1,0:T(8,128)(2,1)S(1)} %get-tuple-element.66), channel_id=1, source_target_pairs={{0,24},{1,25},{2,26},{3,27},{4,28},{5,29},{6,30},{7,31},{8,0},{9,1... | collective-permute-start | bytes 442376 | tf_op jit(solution)/shard_map/ppermute | solution.py:50
  (107 other events, 2035.6 us)
